TPU v7x, 32 devices: a whole 2x2x4 slice. The times are simulated.
32 devices in a mesh: rep: 2 (over x), asset: 8 (over z, y), sample: 2 (over core).
Axes of the slice: x: 2, y: 2, z: 4, core: 2. Of those that a mesh axis runs over, the one named last changes fastest.
Arguments:
- samples: float32 [8, 1024, 32768], P(('rep', 'sample'), None, 'asset'), parts along dimension 0, may hold values from -40 to 40, as said below
- start_panel: float32 [32768, 128], P('asset'), may hold values from -6 to 6
Outputs:
- local_panels: float32 [8, 32768, 128], P(('rep', 'sample'), 'asset'), parts along dimension 0
- subspace: float32 [65536, 128], P(('rep', 'asset')), parts along dimension 0
There are 2 independent parts, one for each index of `rep`. A program takes and returns all parts, laid end to end along the dimension named above; an argument that names none is the same for every part. Nothing has to cross between parts.
Inputs may be any that keep to these rules, and one draw needn't show every extreme that they name: `samples`: returns of each asset with an asset-specific volatility.
All inputs are finite; a program needn't handle non-finite values.
Results may differ from a plain program's by a relative error of at most 0.0003.
Values sent between devices are 32-bit elements; how exact they have to be, the bound alone decides.
No kernel may reach another device: no remote copies, remote signals or barrier semaphores. Data moves between devices by JAX's collectives and lax.ppermute only.
A program may use at most 192 MiB of HBM per device.

v0:
```python
import jax
import jax.numpy as jnp
from jax import lax
from jax.sharding import PartitionSpec as P

LOCAL_ITERS = 2
FINAL_ITERS = 4


HIGH = lax.Precision.HIGHEST


def orthonormal(expanded_panel, gram_matrix):
    cholesky_factor = jnp.linalg.cholesky(gram_matrix)
    solved = jax.scipy.linalg.solve_triangular(
        cholesky_factor, jnp.swapaxes(expanded_panel, -1, -2), lower=True
    )
    return jnp.swapaxes(solved, -1, -2)


def shards(samples, start_panel):
    count_local = samples.shape[0]
    width_all = start_panel.shape[0] * lax.axis_size("asset")
    groups_all = count_local * lax.axis_size("sample")
    panels = jnp.broadcast_to(start_panel, (count_local,) + start_panel.shape)
    for iteration in range(LOCAL_ITERS):
        partial_value = jnp.einsum("gsa,gak->gsk", samples, panels, precision=HIGH)
        scores = lax.psum(partial_value, "asset")
        expanded = jnp.einsum("gsa,gsk->gak", samples, scores, precision=HIGH)
        gram_matrix = (
            lax.psum(jnp.einsum("gak,gal->gkl", expanded, expanded, precision=HIGH), "asset")
            / width_all
        )
        panels = orthonormal(expanded, gram_matrix)
    subspace = start_panel
    gathered = lax.all_gather(panels, "sample", axis=0, tiled=True)
    for iteration in range(FINAL_ITERS):
        correlations = lax.psum(
            jnp.einsum("gak,al->gkl", gathered, subspace, precision=HIGH), "asset"
        )
        averaged = jnp.einsum("gak,gkl->al", gathered, correlations, precision=HIGH) / groups_all
        gram_matrix = (
            lax.psum(jnp.einsum("ak,al->kl", averaged, averaged, precision=HIGH), "asset")
            / width_all
        )
        subspace = orthonormal(averaged, gram_matrix)
    return (panels, subspace)


def solution(mesh):
    placed = (P(("rep", "sample"), None, "asset"), P("asset", None))
    return jax.shard_map(
        shards,
        mesh=mesh,
        in_specs=placed,
        out_specs=(P(("rep", "sample"), "asset", None), P(("rep", "asset"), None)),
        check_vma=False,
    )
```

profile of v0, /device:TPU:0, one launch (start us, length us, event | category | flops | bytes accessed | tf_op | source)
XLA Modules:
  0.0 1376.8 jit_solution(14977466670297829264)
XLA Ops:
  8.8 30.8 %fusion.10 = f32[2,1024,128]{2,1,0:T(8,128)} fusion(f32[2,1024,4096]{2,1,0:T(8,128)} %param.8, f32[4096,128]{1,0:T(8,128)S(1)} %copy-done), kind=kOutput, calls=%fused_computation.19 | convolution fusion | flops 12884901888 | bytes 36700160 | tf_op jit(solution)/shard_map/gsa,gak->gsk/dot_general | solution.py:27
  39.8 80.7 %all-reduce.13.cloned.1.call-done = f32[2,1024,128]{2,1,0:T(8,128)} async-done(((f32[2,1024,128]{2,1,0:T(8,128)}), f32[2,1024,128]{2,1,0:T(8,128)}) %all-reduce.13.cloned.1.call-update) | async-done | bytes 1048592 | tf_op jit(solution)/shard_map/psum | solution.py:28
  120.5 23.3 %fusion.29 = f32[2,128,4096]{2,1,0:T(8,128)} fusion(f32[2,1024,128]{2,1,0:T(8,128)} %all-reduce.13.cloned.1.call-done, f32[2,1024,4096]{2,1,0:T(8,128)} %param.8), kind=kOutput, calls=%fused_computation.71 | convolution fusion | flops 12884901888 | bytes 38797312 | tf_op jit(solution)/shard_map/gsa,gsk->gak/dot_general | solution.py:29
  152.4 69.0 %all-reduce.15.cloned.1.call-done = f32[2,128,128]{1,2,0:T(8,128)} async-done(((f32[2,128,128]{1,2,0:T(8,128)}), f32[2,128,128]{1,2,0:T(8,128)}) %all-reduce.15.cloned.1.call-update) | async-done | bytes 131088 | tf_op jit(solution)/shard_map/psum | solution.py:31
  223.4 23.5 %custom-call.16 = f32[2,128,128]{2,1,0:T(8,128)S(1)} custom-call(f32[2,128,128]{2,1,0:T(8,128)S(1)} %fusion.16), custom_call_target="Cholesky" | custom-call | tf_op jit(solution)/shard_map/jit(cholesky)/cholesky | solution.py:14
  247.1 19.7 %custom-call.17 = f32[2,1,128,128]{2,3,1,0:T(8,128)S(1)} custom-call(f32[2,1,128,128]{3,2,1,0:T(8,128)S(1)} %select_bitcast_fusion.1), custom_call_target="InvertDiagBlocksLowerTriangular" | custom-call | tf_op jit(solution)/shard_map/jit(_solve_triangular)/vmap()/triangular_solve | solution.py:15
  274.6 39.8 %convolution_bitcast_fusion.9 = f32[2,1024,128]{1,2,0:T(8,128)} fusion(f32[2,128,4096]{2,1,0:T(8,128)} %fusion.14, f32[2,1024,4096]{2,1,0:T(8,128)} %param.8), kind=kOutput, calls=%fused_computation.21 | convolution fusion | flops 12884901888 | bytes 38797312 | tf_op jit(solution)/shard_map/gsa,gak->gsk/dot_general | solution.py:27
  314.5 77.4 %all-reduce.17.cloned.1.call-done = f32[2,1024,128]{1,2,0:T(8,128)} async-done(((f32[2,1024,128]{1,2,0:T(8,128)}), f32[2,1024,128]{1,2,0:T(8,128)}) %all-reduce.17.cloned.1.call-update) | async-done | bytes 1048592 | tf_op jit(solution)/shard_map/psum | solution.py:28
  391.9 23.8 %fusion.31 = f32[2,128,4096]{2,1,0:T(8,128)} fusion(f32[2,1024,128]{1,2,0:T(8,128)} %all-reduce.17.cloned.1.call-done, f32[2,1024,4096]{2,1,0:T(8,128)} %param.8), kind=kOutput, calls=%fused_computation.73 | convolution fusion | flops 12884901888 | bytes 38797312 | tf_op jit(solution)/shard_map/gsa,gsk->gak/dot_general | solution.py:29
  424.0 69.3 %all-reduce.19.cloned.1.call-done = f32[2,128,128]{1,2,0:T(8,128)} async-done(((f32[2,128,128]{1,2,0:T(8,128)}), f32[2,128,128]{1,2,0:T(8,128)}) %all-reduce.19.cloned.1.call-update) | async-done | bytes 131088 | tf_op jit(solution)/shard_map/psum | solution.py:31
  495.3 23.6 %custom-call.18 = f32[2,128,128]{2,1,0:T(8,128)S(1)} custom-call(f32[2,128,128]{2,1,0:T(8,128)S(1)} %fusion.13), custom_call_target="Cholesky" | custom-call | tf_op jit(solution)/shard_map/jit(cholesky)/cholesky | solution.py:14
  519.2 19.7 %custom-call.19 = f32[2,1,128,128]{2,3,1,0:T(8,128)S(1)} custom-call(f32[2,1,128,128]{3,2,1,0:T(8,128)S(1)} %select_bitcast_fusion), custom_call_target="InvertDiagBlocksLowerTriangular" | custom-call | tf_op jit(solution)/shard_map/jit(_solve_triangular)/vmap()/triangular_solve | solution.py:15
  552.4 19.2 %all-gather.2.cloned.1.call-done = f32[4,4096,128]{2,1,0:T(8,128)} async-done(((f32[2,4096,128]{2,1,0:T(8,128)}), f32[4,4096,128]{2,1,0:T(8,128)}) %all-gather.2.cloned.1.call-update) | async-done | bytes 8388624 | tf_op jit(solution)/shard_map/all_gather | solution.py:36
  571.6 16.4 %fusion.8 = f32[4,128,128]{2,1,0:T(8,128)} fusion(f32[4,4096,128]{2,1,0:T(8,128)} %all-gather.2.cloned.1.call-done, f32[4096,128]{1,0:T(8,128)S(1)} %copy-done), kind=kOutput, calls=%fused_computation.17 | convolution fusion | flops 3221225472 | bytes 10747904 | tf_op jit(solution)/shard_map/gak,al->gkl/dot_general | solution.py:39
  588.0 71.8 %all-reduce.21.cloned.1.call-done = f32[4,128,128]{2,1,0:T(8,128)} async-done(((f32[4,128,128]{2,1,0:T(8,128)}), f32[4,128,128]{2,1,0:T(8,128)}) %all-reduce.21.cloned.1.call-update) | async-done | bytes 262160 | tf_op jit(solution)/shard_map/psum | solution.py:38
  675.4 67.4 %all-reduce.23.cloned.1.call-done = f32[128,128]{0,1:T(8,128)} async-done(((f32[128,128]{0,1:T(8,128)}), f32[128,128]{0,1:T(8,128)}) %all-reduce.23.cloned.1.call-update) | async-done | bytes 65552 | tf_op jit(solution)/shard_map/psum | solution.py:43
  787.3 70.6 %all-reduce.25.cloned.1.call-done = f32[4,128,128]{2,1,0:T(8,128)} async-done(((f32[4,128,128]{2,1,0:T(8,128)}), f32[4,128,128]{2,1,0:T(8,128)}) %all-reduce.25.cloned.1.call-update) | async-done | bytes 262160 | tf_op jit(solution)/shard_map/psum | solution.py:38
  873.2 67.6 %all-reduce.27.cloned.1.call-done = f32[128,128]{0,1:T(8,128)} async-done(((f32[128,128]{0,1:T(8,128)}), f32[128,128]{0,1:T(8,128)}) %all-reduce.27.cloned.1.call-update) | async-done | bytes 65552 | tf_op jit(solution)/shard_map/psum | solution.py:43
  968.9 16.5 %fusion.36 = f32[4,128,128]{2,1,0:T(8,128)} fusion(f32[4,4096,128]{2,1,0:T(8,128)} %all-gather.2.cloned.1.call-done, f32[128,4096,1]{1,0,2:T(8,128)S(1)} %convolution_bitcast_fusion.5), kind=kOutput, calls=%fused_computation.78 | convolution fusion | flops 3221225472 | bytes 10747904 | tf_op jit(solution)/shard_map/gak,al->gkl/dot_general | solution.py:39
  985.4 70.6 %all-reduce.29.cloned.1.call-done = f32[4,128,128]{2,1,0:T(8,128)} async-done(((f32[4,128,128]{2,1,0:T(8,128)}), f32[4,128,128]{2,1,0:T(8,128)}) %all-reduce.29.cloned.1.call-update) | async-done | bytes 262160 | tf_op jit(solution)/shard_map/psum | solution.py:38
  1071.6 67.7 %all-reduce.31.cloned.1.call-done = f32[128,128]{0,1:T(8,128)} async-done(((f32[128,128]{0,1:T(8,128)}), f32[128,128]{0,1:T(8,128)}) %all-reduce.31.cloned.1.call-update) | async-done | bytes 65552 | tf_op jit(solution)/shard_map/psum | solution.py:43
  1167.4 16.4 %fusion.38 = f32[4,128,128]{2,1,0:T(8,128)} fusion(f32[4,4096,128]{2,1,0:T(8,128)} %all-gather.2.cloned.1.call-done, f32[128,4096,1]{1,0,2:T(8,128)S(1)} %convolution_bitcast_fusion.3), kind=kOutput, calls=%fused_computation.80 | convolution fusion | flops 3221225472 | bytes 10747904 | tf_op jit(solution)/shard_map/gak,al->gkl/dot_general | solution.py:39
  1183.8 70.6 %all-reduce.33.cloned.1.call-done = f32[4,128,128]{2,1,0:T(8,128)} async-done(((f32[4,128,128]{2,1,0:T(8,128)}), f32[4,128,128]{2,1,0:T(8,128)}) %all-reduce.33.cloned.1.call-update) | async-done | bytes 262160 | tf_op jit(solution)/shard_map/psum | solution.py:38
  1269.5 67.9 %all-reduce.35.cloned.1.call-done = f32[128,128]{0,1:T(8,128)} async-done(((f32[128,128]{0,1:T(8,128)}), f32[128,128]{0,1:T(8,128)}) %all-reduce.35.cloned.1.call-update) | async-done | bytes 65552 | tf_op jit(solution)/shard_map/psum | solution.py:43
  (101 shorter events, 239.0 us)
Async XLA Ops:
  7.2 1.6 copy-start
  7.2 113.3 %all-reduce.13.cloned.1.call-start = ((), (), s32[]{:S(2)}) async-start(), calls=%async_computation | async-start | bytes 2097152 | tf_op jit(solution)/shard_map/psum | solution.py:28
  39.6 181.9 %all-reduce.15.cloned.1.call-start = ((), (), s32[]{:S(2)}) async-start(), calls=%async_computation.1 | async-start | bytes 262144 | tf_op jit(solution)/shard_map/psum | solution.py:31
  152.1 239.9 %all-reduce.17.cloned.1.call-start = ((), (), s32[]{:S(2)}) async-start(), calls=%async_computation.2 | async-start | bytes 2097152 | tf_op jit(solution)/shard_map/psum | solution.py:28
  314.5 178.9 %all-reduce.19.cloned.1.call-start = ((), (), s32[]{:S(2)}) async-start(), calls=%async_computation.3 | async-start | bytes 262144 | tf_op jit(solution)/shard_map/psum | solution.py:31
  424.0 147.6 %all-gather.2.cloned.1.call-start = ((), (), s32[]{:S(2)}) async-start(), calls=%async_computation.4 | async-start | bytes 12582912 | tf_op jit(solution)/shard_map/all_gather | solution.py:36
  552.3 107.6 %all-reduce.21.cloned.1.call-start = ((), (), s32[]{:S(2)}) async-start(), calls=%async_computation.5 | async-start | bytes 524288 | tf_op jit(solution)/shard_map/psum | solution.py:38
  588.0 154.9 %all-reduce.23.cloned.1.call-start = ((), (), s32[]{:S(2)}) async-start(), calls=%async_computation.6 | async-start | bytes 131072 | tf_op jit(solution)/shard_map/psum | solution.py:43
  669.4 1.3 copy-start.1
  674.9 183.0 %all-reduce.25.cloned.1.call-start = ((), (), s32[]{:S(2)}) async-start(), calls=%async_computation.7 | async-start | bytes 524288 | tf_op jit(solution)/shard_map/psum | solution.py:38
  787.3 153.5 %all-reduce.27.cloned.1.call-start = ((), (), s32[]{:S(2)}) async-start(), calls=%async_computation.8 | async-start | bytes 131072 | tf_op jit(solution)/shard_map/psum | solution.py:43
  867.4 1.3 copy-start.2
  872.9 183.1 %all-reduce.29.cloned.1.call-start = ((), (), s32[]{:S(2)}) async-start(), calls=%async_computation.9 | async-start | bytes 524288 | tf_op jit(solution)/shard_map/psum | solution.py:38
  985.4 153.9 %all-reduce.31.cloned.1.call-start = ((), (), s32[]{:S(2)}) async-start(), calls=%async_computation.10 | async-start | bytes 131072 | tf_op jit(solution)/shard_map/psum | solution.py:43
  1065.8 1.3 copy-start.3
  1071.3 183.1 %all-reduce.33.cloned.1.call-start = ((), (), s32[]{:S(2)}) async-start(), calls=%async_computation.11 | async-start | bytes 524288 | tf_op jit(solution)/shard_map/psum | solution.py:38
  1183.8 153.6 %all-reduce.35.cloned.1.call-start = ((), (), s32[]{:S(2)}) async-start(), calls=%async_computation.12 | async-start | bytes 131072 | tf_op jit(solution)/shard_map/psum | solution.py:43
  1264.0 1.3 copy-start.4
Sparse Core Ops, SparseCore 0:
  39.7 80.7 all-reduce.12
  152.2 69.1 all-reduce.14
  314.6 77.3 all-reduce.16
  424.1 69.1 all-reduce.18
  552.4 19.1 all-gather.1
  588.1 71.7 all-reduce.20
  675.0 67.7 all-reduce.22
  787.4 70.4 all-reduce.24
  873.0 67.6 all-reduce.26
  985.5 70.5 all-reduce.28
  1071.5 67.7 all-reduce.30
  1183.9 70.4 all-reduce.32
  1269.6 67.7 all-reduce.34
where the time goes:
time: 1380 us
  waiting for transfers between devices  870 us (63%)
  matrix products  286 us (21%)
  other arithmetic  189 us (14%)
  local copies, waits for them, and re-layouts  15.8 us (1%)
  between operations  14.6 us (1%)
    psum x4, waiting for transfers between devices, shards(): lax.psum(jnp.einsum('gak,al->gkl', gathered, subspace, precision=HIGH), '...  284 us
    psum x4, waiting for transfers between devices, shards(): lax.psum(jnp.einsum('ak,al->kl', averaged, averaged, precision=HIGH), 'as...  271 us
    psum x2, waiting for transfers between devices, shards(): scores = lax.psum(partial_value, 'asset')  158 us
    psum x2, waiting for transfers between devices, shards(): lax.psum(jnp.einsum('gak,gal->gkl', expanded, expanded, precision=HIGH),...  138 us
    another operation x19, other arithmetic, orthonormal(): cholesky_factor = jnp.linalg.cholesky(gram_matrix)  97 us
    another operation x13, other arithmetic, orthonormal(): jax.scipy.linalg.solve_triangular(cholesky_factor, jnp.swapaxes(expanded_...  81.2 us
    dot_general x2, matrix products, shards(): partial_value = jnp.einsum('gsa,gak->gsk', samples, panels, precision=HIGH)  70.6 us
    dot_general x4, matrix products, shards(): jnp.einsum('gak,al->gkl', gathered, subspace, precision=HIGH)  65.5 us
  transfers between devices with their start and end apart: 13, of which 13 were waited for; matrix products, arithmetic and copies ran while one was open for 0% of the time, Pallas kernels for 0%

commit v1 on v0

v1 whole, which is shorter than its diff:
```python
import functools

import jax
import jax.numpy as jnp
from jax import lax
from jax.experimental import pallas as pl
from jax.experimental.pallas import tpu as pltpu
from jax.sharding import PartitionSpec as P

LOCAL_ITERS = 2
FINAL_ITERS = 4


HIGH = lax.Precision.HIGHEST
THREE = lax.Precision.HIGH
TILE = 8
PANEL = 4


def dot_exact(left, right, dims):
    return lax.dot_general(
        left, right, (dims, ((), ())), precision=HIGH, preferred_element_type=jnp.float32
    )


def inverse_factors(matrices):
    size = matrices[0].shape[0]
    blocks = size // TILE
    full = (TILE, size)
    sublane = lax.broadcasted_iota(jnp.int32, full, 0)
    lane = lax.broadcasted_iota(jnp.int32, full, 1)
    left, right = [], []
    for matrix in matrices:
        symmetric = 0.5 * (matrix + matrix.T)
        left.append([symmetric[TILE * i : TILE * (i + 1)] for i in range(blocks)])
        right.append(
            [jnp.where(lane == sublane + TILE * i, 1.0, 0.0) for i in range(blocks)]
        )
    along = lambda block, row: jnp.broadcast_to(block[row : row + 1], full)
    across = lambda block, column: jnp.broadcast_to(block[:, column : column + 1], full)
    for panel in range(0, blocks, PANEL):
        last = panel + PANEL
        for j in range(panel, last):
            for a, b in zip(left, right):
                columns = [across(a[j], TILE * j + k) for k in range(TILE)]
                d = [[along(columns[k], i) for k in range(i + 1)] for i in range(TILE)]
                scale = []
                for k in range(TILE):
                    scale.append(lax.rsqrt(d[k][k]))
                    for i in range(k + 1, TILE):
                        d[i][k] = d[i][k] * scale[k]
                    for i in range(k + 1, TILE):
                        for m in range(k + 1, i + 1):
                            d[i][m] = d[i][m] - d[i][k] * d[m][k]

                def substitute(parts):
                    for k in range(TILE):
                        for m in range(k):
                            parts[k] = parts[k] - d[k][m] * parts[m]
                        parts[k] = parts[k] * scale[k]
                    return parts

                rows_a = substitute([along(a[j], k) for k in range(TILE)])
                rows_b = substitute([along(b[j], k) for k in range(TILE)])
                for i in range(j + 1, last):
                    weights = substitute([across(a[i], TILE * j + k) for k in range(TILE)])
                    for k in range(TILE):
                        a[i] = a[i] - weights[k] * rows_a[k]
                        b[i] = b[i] - weights[k] * rows_b[k]

                def gather(rows):
                    block = rows[0]
                    for k in range(1, TILE):
                        block = jnp.where(sublane == k, rows[k], block)
                    return block

                a[j], b[j] = gather(rows_a), gather(rows_b)
        if last < blocks:
            for a, b in zip(left, right):
                top_a = jnp.concatenate(a[panel:last], axis=0)
                top_b = jnp.concatenate(b[panel:last], axis=0)
                change = dot_exact(
                    top_a[:, TILE * last :],
                    jnp.concatenate([top_a, top_b], axis=1),
                    ((0,), (0,)),
                )
                for i in range(last, blocks):
                    rows = change[TILE * (i - last) : TILE * (i - last + 1)]
                    a[i] = a[i] - rows[:, :size]
                    b[i] = b[i] - rows[:, size:]
    return [jnp.concatenate(b, axis=0) for b in right]


def normal_kernel(width_all, first_ref, second_ref, out_ref):
    count = first_ref.shape[0]
    grams = [
        dot_exact(first_ref[g], second_ref[g], ((0,), (0,))) * (1.0 / width_all)
        for g in range(count)
    ]
    for g, inverse in enumerate(inverse_factors(grams)):
        out_ref[g] = dot_exact(second_ref[g], inverse, ((1,), (1,)))


def final_kernel(width_all, gram_ref, start_ref, inverse_ref, out_ref, matrix, block):
    count, _, size = inverse_ref.shape
    at = lambda g: slice(g * size, (g + 1) * size)
    inverses = inverse_factors(
        [gram_ref[at(g), at(g)] * (1.0 / width_all) for g in range(count)]
    )
    for g in range(count):
        inverse_ref[g] = inverses[g]
        block[at(g), :] = dot_exact(inverses[g], start_ref[at(g), :], ((1,), (0,)))
        row = dot_exact(inverses[g], gram_ref[at(g), :], ((1,), (0,)))
        for h in range(count):
            matrix[at(g), at(h)] = dot_exact(row[:, at(h)], inverses[h], ((1,), (1,)))

    def step(_, carry):
        held = block[...] * (1.0 / count)
        product = dot_exact(matrix[...], held, ((1,), (0,)))
        small = dot_exact(held, product, ((0,), (0,))) * (1.0 / width_all)
        (inverse,) = inverse_factors([small])
        out_ref[...] = dot_exact(held, inverse, ((1,), (1,)))
        block[...] = dot_exact(product, inverse, ((1,), (1,)))
        return carry

    lax.fori_loop(0, FINAL_ITERS, step, 0)
    held = [
        dot_exact(inverses[g], out_ref[at(g), :], ((0,), (0,))) for g in range(count)
    ]
    for g in range(count):
        out_ref[at(g), :] = held[g]


def normalise(first, second, width_all):
    return pl.pallas_call(
        functools.partial(normal_kernel, width_all),
        out_shape=jax.ShapeDtypeStruct(second.shape, jnp.float32),
        compiler_params=pltpu.CompilerParams(vmem_limit_bytes=32 * 1024 * 1024),
    )(first, second)


def final_iterations(gram, start, width_all, groups_all):
    size = start.shape[-1]
    return pl.pallas_call(
        functools.partial(final_kernel, width_all),
        out_shape=(
            jax.ShapeDtypeStruct((groups_all, size, size), jnp.float32),
            jax.ShapeDtypeStruct((groups_all * size, size), jnp.float32),
        ),
        scratch_shapes=[
            pltpu.VMEM((groups_all * size, groups_all * size), jnp.float32),
            pltpu.VMEM((groups_all * size, size), jnp.float32),
        ],
        compiler_params=pltpu.CompilerParams(vmem_limit_bytes=32 * 1024 * 1024),
    )(gram, start)


def bit_orders(bits):
    return [list(range(bits)), list(range(1, bits)) + [0]]


def total_over_assets(value):
    count, cores = lax.axis_size("asset"), lax.axis_size("sample")
    bits = count.bit_length() - 1
    orders = bit_orders(bits)
    place, core = lax.axis_index("asset"), lax.axis_index("sample")

    def exchange(held, stage):
        pairs = [
            (a * cores + c, (a ^ (1 << orders[c % 2][stage])) * cores + c)
            for a in range(count)
            for c in range(cores)
        ]
        return lax.ppermute(held, ("asset", "sample"), pairs)

    def my_bit(stage):
        bit = jnp.where(core % 2 == 0, orders[0][stage], orders[1][stage])
        return (place >> bit) & 1

    shape = value.shape
    held = value.reshape((-1, shape[-1]))
    for stage in range(bits):
        halves = held.reshape((2, -1, shape[-1]))
        mine = my_bit(stage)
        sent = lax.dynamic_index_in_dim(halves, 1 - mine, 0, keepdims=False)
        kept = lax.dynamic_index_in_dim(halves, mine, 0, keepdims=False)
        held = kept + exchange(sent, stage)
    for stage in reversed(range(bits)):
        other = exchange(held, stage)
        mine = my_bit(stage)
        held = jnp.where(
            mine == 0,
            jnp.concatenate([held, other], axis=0),
            jnp.concatenate([other, held], axis=0),
        )
    return held.reshape(shape)


def total_direct(value):
    count = lax.axis_size("asset")
    place = lax.axis_index("asset")
    shape = value.shape
    parts = value.reshape((count, -1, shape[-1]))
    part = lambda index: lax.dynamic_index_in_dim(parts, index % count, 0, keepdims=False)
    ring = lambda held, d: lax.ppermute(
        held, "asset", [(a, (a + d) % count) for a in range(count)]
    )
    total = part(place)
    for received in [ring(part(place + d), d) for d in range(1, count)]:
        total = total + received
    arrived = [total] + [ring(total, d) for d in range(1, count)]
    turned = jnp.stack(arrived[::-1] + arrived[::-1], axis=0)
    whole = lax.dynamic_slice_in_dim(turned, count - 1 - place, count, axis=0)
    return whole.reshape(shape)


def shards(samples, start_panel):
    count_local = samples.shape[0]
    rows, size = start_panel.shape
    width_all = rows * lax.axis_size("asset")
    cores = lax.axis_size("sample")
    groups_all = count_local * cores
    core = lax.axis_index("sample")
    scores = total_over_assets(
        jnp.einsum("gsa,ak->gsk", samples, start_panel, precision=THREE)
    )
    first_scores = scores
    for iteration in range(LOCAL_ITERS - 1):
        expanded = jnp.einsum("gsa,gsk->gak", samples, scores, precision=THREE)
        following = total_direct(
            jnp.einsum("gsa,gak->gsk", samples, expanded, precision=THREE)
        )
        scores = normalise(scores, following, width_all)
    expanded = jnp.einsum("gsa,gsk->gak", samples, scores, precision=THREE)
    start = jnp.einsum("gsk,gsl->gkl", scores, first_scores, precision=HIGH)

    gathered = lax.all_gather(expanded, "sample", axis=0, tiled=True)
    start = lax.all_gather(start, "sample", axis=0, tiled=True)
    part = rows // cores
    half = lax.dynamic_slice_in_dim(gathered, core * part, part, axis=1)
    flat = jnp.swapaxes(half, 0, 1).reshape((part, groups_all * size))
    partial_gram = jnp.einsum("ai,aj->ij", flat, flat, precision=HIGH)
    pairs = [(c, (c + 1) % cores) for c in range(cores)]
    shared = partial_gram
    passing = partial_gram
    for _ in range(cores - 1):
        passing = lax.ppermute(passing, "sample", pairs)
        shared = shared + passing
    gram = total_direct(shared)
    inverses, weights = final_iterations(
        gram, start.reshape((groups_all * size, size)), width_all, groups_all
    )
    own = lax.dynamic_slice_in_dim(inverses, core * count_local, count_local, axis=0)
    panels = jnp.einsum("gak,glk->gal", expanded, own, precision=HIGH)
    subspace = jnp.einsum(
        "gak,gkl->al", gathered, weights.reshape((groups_all, size, size)), precision=HIGH
    )
    return (panels, subspace)


def solution(mesh):
    placed = (P(("rep", "sample"), None, "asset"), P("asset", None))
    return jax.shard_map(
        shards,
        mesh=mesh,
        in_specs=placed,
        out_specs=(P(("rep", "sample"), "asset", None), P(("rep", "asset"), None)),
        check_vma=False,
    )
```

time: 1380 us -> 387 us (0.28)
  waiting for transfers between devices: 870 us -> 107 us
  other arithmetic: 189 us -> 2.73 us
  matrix products: 286 us -> 108 us
  starting transfers between devices: 1.81 us -> 77.3 us
  Pallas kernels: 0 us -> 49 us
    psum x12 -> x0, waiting for transfers between devices: 851 us -> none  [the longest x4 284 us: shards(): lax.psum(jnp.einsum('gak,al->gkl', gathered, subspace, precision=HIGH), '...]
    another operation x32 -> x0, other arithmetic: 178 us -> none  [the longest x19 97 us: orthonormal(): cholesky_factor = jnp.linalg.cholesky(gram_matrix)]
    dot_general x18 -> x8, matrix products: 255 us -> 108 us  [the longest x2 37.9 us: shards(): expanded = jnp.einsum('gsa,gsk->gak', samples, scores, precision=THREE)]
    ppermute x0 -> x35, waiting for transfers between devices: none -> 85.5 us  [the longest x28 49.4 us: total_direct(): lax.ppermute(held, 'asset', [(a, (a + d) % count) for a in range(count)])]
    ppermute x0 -> x35, starting transfers between devices: none -> 77.2 us  [the longest x28 58.2 us: total_direct(): lax.ppermute(held, 'asset', [(a, (a + d) % count) for a in range(count)])]
    pallas_call x0 -> x2, Pallas kernels: none -> 49 us  [the longest x1 41.4 us: final_iterations(): pl.pallas_call(functools.partial(final_kernel, width_all), out_shape=(jax...]
    another operation x6 -> x0, matrix products: 31.1 us -> none  [orthonormal(): jax.scipy.linalg.solve_triangular(cholesky_factor, jnp.swapaxes(expanded_...]
  transfers between devices with their start and end apart: 13 -> 36, of which waited for: 13 -> 17; matrix products, arithmetic and copies ran while one was open for 0% -> 1% of each run, Pallas kernels for 0% -> 0%
where the time goes in v1:
time: 387 us; the launch traced here: 380 us
  matrix products  108 us (28%)
  waiting for transfers between devices  107 us (28%)
  starting transfers between devices  77.3 us (20%)
  Pallas kernels  49 us (13%)
  local copies, waits for them, and re-layouts  19.6 us (5%)
  between operations  14.7 us (4%)
    ppermute x28, starting transfers between devices, total_direct(): lax.ppermute(held, 'asset', [(a, (a + d) % count) for a in range(count)])  58.2 us
    ppermute x28, waiting for transfers between devices, total_direct(): lax.ppermute(held, 'asset', [(a, (a + d) % count) for a in range(count)])  49.4 us
    pallas_call x1, Pallas kernels, final_iterations(): pl.pallas_call(functools.partial(final_kernel, width_all), out_shape=(jax...  41.4 us
    dot_general x2, matrix products, shards(): expanded = jnp.einsum('gsa,gsk->gak', samples, scores, precision=THREE)  37.9 us
    ppermute x6, waiting for transfers between devices, exchange(): return lax.ppermute(held, ('asset', 'sample'), pairs)  33.6 us
    dot_general x1, matrix products, shards(): jnp.einsum('gsa,gak->gsk', samples, expanded, precision=THREE)  22.8 us
    all_gather x1, waiting for transfers between devices, shards(): gathered = lax.all_gather(expanded, 'sample', axis=0, tiled=True)  21.6 us
    ppermute x6, starting transfers between devices, exchange(): return lax.ppermute(held, ('asset', 'sample'), pairs)  18.8 us
  transfers between devices with their start and end apart: 36, of which 17 were waited for; matrix products, arithmetic and copies ran while one was open for 1% of the time, Pallas kernels for 0%

profile of v1, /device:TPU:0, one launch (start us, length us, event | category | flops | bytes accessed | tf_op | source)
XLA Modules:
  0.0 380.0 jit_solution(2359555276550632496)
XLA Ops:
  8.8 17.2 %fusion = f32[2,1024,128]{2,1,0:T(8,128)S(1)} fusion(f32[2,1024,4096]{2,1,0:T(8,128)} %param.2, f32[4096,128]{1,0:T(8,128)S(1)} %copy-done), kind=kOutput, calls=%fused_computation.1 | convolution fusion | flops 6442450944 | bytes 36700160 | tf_op jit(solution)/shard_map/gsa,ak->gsk/dot_general | solution.py:225
  29.0 7.2 %collective-permute-done = f32[1024,128]{1,0:T(8,128)S(1)} collective-permute-done((f32[1024,128]{1,0:T(8,128)S(1)}, f32[1024,128]{1,0:T(8,128)S(1)}, u32[]{:S(2)}, u32[]{:S(2)}) %collective-permute-start) | collective-permute-done | bytes 524320 | tf_op jit(solution)/shard_map/ppermute | solution.py:174
  38.4 5.7 %collective-permute-done.1 = f32[512,128]{1,0:T(8,128)S(1)} collective-permute-done((f32[512,128]{1,0:T(8,128)S(1)}, f32[512,128]{1,0:T(8,128)S(1)}, u32[]{:S(2)}, u32[]{:S(2)}) %collective-permute-start.1) | collective-permute-done | bytes 262176 | tf_op jit(solution)/shard_map/ppermute | solution.py:174
  57.6 5.5 %collective-permute-start.4 = (f32[512,128]{1,0:T(8,128)S(1)}, f32[512,128]{1,0:T(8,128)S(1)}, u32[]{:S(2)}, u32[]{:S(2)}) collective-permute-start(f32[512,128]{1,0:T(8,128)S(1)} %maximum_select_fusion.2), channel_id=1, source_target_pairs={{0,4},{1,9},{2,6},{3,11},{4,0},{5,13},{6,2},{7,15},{8,12},{9,1},{1... | collective-permute-start | bytes 786440 | tf_op jit(solution)/shard_map/ppermute | solution.py:174
  63.1 6.3 %collective-permute-done.4 = f32[512,128]{1,0:T(8,128)S(1)} collective-permute-done((f32[512,128]{1,0:T(8,128)S(1)}, f32[512,128]{1,0:T(8,128)S(1)}, u32[]{:S(2)}, u32[]{:S(2)}) %collective-permute-start.4) | collective-permute-done | bytes 262176 | tf_op jit(solution)/shard_map/ppermute | solution.py:174
  70.9 7.7 %collective-permute-done.5 = f32[1024,128]{1,0:T(8,128)S(1)} collective-permute-done((f32[1024,128]{1,0:T(8,128)S(1)}, f32[1024,128]{1,0:T(8,128)S(1)}, u32[]{:S(2)}, u32[]{:S(2)}) %collective-permute-start.5) | collective-permute-done | bytes 524320 | tf_op jit(solution)/shard_map/ppermute | solution.py:174
  78.7 18.9 %fusion.17 = f32[2,128,4096]{2,1,0:T(8,128)} fusion(f32[2,1024,128]{2,1,0:T(8,128)S(1)} %bitcast.150, f32[2,1024,4096]{2,1,0:T(8,128)} %param.2), kind=kOutput, calls=%fused_computation.79 | convolution fusion | flops 6442450944 | bytes 38797312 | tf_op jit(solution)/shard_map/gsa,gsk->gak/dot_general | solution.py:229
  97.6 22.8 %convolution_bitcast_fusion.1 = f32[2,1024,128]{1,2,0:T(8,128)S(1)} fusion(f32[2,128,4096]{2,1,0:T(8,128)} %fusion.17, f32[2,1024,4096]{2,1,0:T(8,128)} %param.2), kind=kOutput, calls=%fused_computation.3 | convolution fusion | flops 6442450944 | bytes 38797312 | tf_op jit(solution)/shard_map/gsa,gak->gsk/dot_general | solution.py:231
  122.4 5.0 %collective-permute-start.12 = (f32[256,128]{1,0:T(8,128)S(1)}, f32[256,128]{1,0:T(8,128)S(1)}, u32[]{:S(2)}, u32[]{:S(2)}) collective-permute-start(f32[256,128]{1,0:T(8,128)S(1)} %get-tuple-element.14), channel_id=1, source_target_pairs={{0,14},{2,0},{4,2},{6,4},{8,6},{10,8},{12,10},{14,12},{1,15},{3,1}... | collective-permute-start | bytes 393224 | tf_op jit(solution)/shard_map/ppermute | solution.py:205
  136.7 8.7 %collective-permute-done.9 = f32[256,128]{1,0:T(8,128)S(1)} collective-permute-done((f32[256,128]{1,0:T(8,128)S(1)}, f32[256,128]{1,0:T(8,128)S(1)}, u32[]{:S(2)}, u32[]{:S(2)}) %collective-permute-start.9) | collective-permute-done | bytes 131104 | tf_op jit(solution)/shard_map/ppermute | solution.py:205
  155.2 5.4 %collective-permute-done.14 = f32[256,128]{1,0:T(8,128)S(1)} collective-permute-done((f32[256,128]{1,0:T(8,128)S(1)}, f32[256,128]{1,0:T(8,128)S(1)}, u32[]{:S(2)}, u32[]{:S(2)}) %collective-permute-start.14) | collective-permute-done | bytes 131104 | tf_op jit(solution)/shard_map/ppermute | solution.py:205
  160.7 6.7 %collective-permute-start.15 = (f32[256,128]{1,0:T(8,128)S(1)}, f32[256,128]{1,0:T(8,128)S(1)}, u32[]{:S(2)}, u32[]{:S(2)}) collective-permute-start(f32[256,128]{1,0:T(8,128)S(1)} %fusion.13), channel_id=1, source_target_pairs={{0,10},{2,12},{4,14},{6,0},{8,2},{10,4},{12,6},{14,8},{1,11},{3,13... | collective-permute-start | bytes 393224 | tf_op jit(solution)/shard_map/ppermute | solution.py:205
  172.0 7.5 %shard_map.41 = f32[2,1024,128]{2,1,0:T(8,128)S(1)} custom-call(f32[2,1024,128]{2,1,0:T(8,128)S(1)} %bitcast.151, f32[2,1024,128]{2,1,0:T(8,128)S(1)} %bitcast.153), custom_call_target="tpu_custom_call" | custom-call | tf_op jit(solution)/shard_map/pallas_call | solution.py:135
  179.6 19.0 %fusion.18 = f32[2,128,4096]{2,1,0:T(8,128)} fusion(f32[2,1024,128]{2,1,0:T(8,128)S(1)} %shard_map.41, f32[2,1024,4096]{2,1,0:T(8,128)} %param.2), kind=kOutput, calls=%fused_computation.80 | convolution fusion | flops 6442450944 | bytes 38797312 | tf_op jit(solution)/shard_map/gsa,gsk->gak/dot_general | solution.py:234
  198.6 5.6 %copy.22 = f32[2,4096,128]{2,1,0:T(8,128)} copy(f32[2,4096,128]{1,2,0:T(8,128)} %bitcast.157) | data formatting | bytes 8388608 | tf_op jit(solution)/shard_map/gsa,gsk->gak/dot_general | solution.py:234
  204.3 21.6 %all-gather.2.cloned.1.call-done = f32[4,4096,128]{2,1,0:T(8,128)} async-done(((f32[2,4096,128]{2,1,0:T(8,128)}), f32[4,4096,128]{2,1,0:T(8,128)}) %all-gather.2.cloned.1.call-update) | async-done | bytes 8388624 | tf_op jit(solution)/shard_map/all_gather | solution.py:237
  230.3 5.5 %copy.30 = f32[4,2048,128]{1,2,0:T(8,128)} copy(f32[4,2048,128]{2,1,0:T(8,128)} %constant_dynamic-slice_fusion.1) | data formatting | bytes 8388608
  235.8 9.5 %fusion.19 = f32[512,512]{1,0:T(8,128)S(1)} fusion(f32[2048,512]{0,1:T(8,128)} %bitcast.158), kind=kOutput, calls=%fused_computation.81 | convolution fusion | flops 6442450944 | bytes 5242880 | tf_op jit(solution)/shard_map/ai,aj->ij/dot_general | solution.py:242
  263.3 14.4 %collective-permute-done.24 = f32[64,512]{1,0:T(8,128)} collective-permute-done((f32[64,512]{1,0:T(8,128)}, f32[64,512]{1,0:T(8,128)}, u32[]{:S(2)}, u32[]{:S(2)}) %collective-permute-start.24) | collective-permute-done | bytes 131104 | tf_op jit(solution)/shard_map/ppermute | solution.py:205
  291.4 7.6 %collective-permute-done.29 = f32[64,512]{1,0:T(8,128)S(1)} collective-permute-done((f32[64,512]{1,0:T(8,128)S(1)}, f32[64,512]{1,0:T(8,128)S(1)}, u32[]{:S(2)}, u32[]{:S(2)}) %collective-permute-start.29) | collective-permute-done | bytes 131104 | tf_op jit(solution)/shard_map/ppermute | solution.py:205
  299.0 8.9 %collective-permute-start.30 = (f32[64,512]{1,0:T(8,128)S(1)}, f32[64,512]{1,0:T(8,128)S(1)}, u32[]{:S(2)}, u32[]{:S(2)}) collective-permute-start(f32[64,512]{1,0:T(8,128)S(1)} %fusion.7), channel_id=1, source_target_pairs={{0,10},{2,12},{4,14},{6,0},{8,2},{10,4},{12,6},{14,8},{1,11},{3,13... | collective-permute-start | bytes 393224 | tf_op jit(solution)/shard_map/ppermute | solution.py:205
  313.0 41.4 %shard_map.42 = (f32[4,128,128]{2,1,0:T(8,128)S(1)}, f32[512,128]{1,0:T(8,128)S(1)}) custom-call(f32[512,512]{1,0:T(8,128)S(1)} %bitcast.154, f32[512,128]{1,0:T(8,128)S(1)} %bitcast.155), custom_call_target="tpu_custom_call" | custom-call | tf_op jit(solution)/shard_map/pallas_call | solution.py:144
  354.4 8.2 %fusion.14 = f32[2,4096,128]{2,1,0:T(8,128)} fusion(f32[2,128,4096]{2,1,0:T(8,128)S(1)} %copy-done.2, f32[4,128,128]{2,1,0:T(8,128)S(1)} %get-tuple-element.4, s32[]{:T(128)S(6)} %select_n.206), kind=kOutput, calls=%fused_computation.58 | convolution fusion | flops 1610612736 | bytes 8519684 | tf_op jit(solution)/shard_map/gak,glk->gal/dot_general | solution.py:254
  362.7 10.3 %convolution_bitcast_fusion = f32[4096,128]{1,0:T(8,128)} fusion(f32[4,4096,128]{2,1,0:T(8,128)} %all-gather.2.cloned.1.call-done, f32[4,128,128]{2,1,0:T(8,128)S(1)} %bitcast.156), kind=kOutput, calls=%fused_computation | convolution fusion | flops 3221225472 | bytes 10747904 | tf_op jit(solution)/shard_map/gak,gkl->al/dot_general | solution.py:255
  (120 shorter events, 88.8 us)
Async XLA Ops:
  7.2 218.7 %all-gather.2.cloned.1.call-start = ((), (), s32[]{:S(2)}) async-start(), calls=%async_computation | async-start | bytes 12582912 | tf_op jit(solution)/shard_map/all_gather | solution.py:237
  26.0 10.2 %collective-permute-start = (f32[1024,128]{1,0:T(8,128)S(1)}, f32[1024,128]{1,0:T(8,128)S(1)}, u32[]{:S(2)}, u32[]{:S(2)}) collective-permute-start(f32[1024,128]{1,0:T(8,128)S(1)} %dynamic-slice_bitcast_fusion), channel_id=1, source_target_pairs={{0,2},{1,5},{2,0},{3,7},{4,6},{5,1},{6,4},{7,3},{8,10},{9,13},{10,... | collective-permute-start | bytes 1572872 | tf_op jit(solution)/shard_map/ppermute | solution.py:174
  57.6 11.7 %collective-permute-start.4 = (f32[512,128]{1,0:T(8,128)S(1)}, f32[512,128]{1,0:T(8,128)S(1)}, u32[]{:S(2)}, u32[]{:S(2)}) collective-permute-start(f32[512,128]{1,0:T(8,128)S(1)} %maximum_select_fusion.2), channel_id=1, source_target_pairs={{0,4},{1,9},{2,6},{3,11},{4,0},{5,13},{6,2},{7,15},{8,12},{9,1},{1... | collective-permute-start | bytes 786440 | tf_op jit(solution)/shard_map/ppermute | solution.py:174
  120.8 11.5 %collective-permute-start.6 = (f32[256,128]{1,0:T(8,128)S(1)}, f32[256,128]{1,0:T(8,128)S(1)}, u32[]{:S(2)}, u32[]{:S(2)}) collective-permute-start(f32[256,128]{1,0:T(8,128)S(1)} %get-tuple-element.13), channel_id=1, source_target_pairs={{0,2},{2,4},{4,6},{6,8},{8,10},{10,12},{12,14},{14,0},{1,3},{3,5},... | collective-permute-start | bytes 393224 | tf_op jit(solution)/shard_map/ppermute | solution.py:205
  122.4 10.3 %collective-permute-start.12 = (f32[256,128]{1,0:T(8,128)S(1)}, f32[256,128]{1,0:T(8,128)S(1)}, u32[]{:S(2)}, u32[]{:S(2)}) collective-permute-start(f32[256,128]{1,0:T(8,128)S(1)} %get-tuple-element.14), channel_id=1, source_target_pairs={{0,14},{2,0},{4,2},{6,4},{8,6},{10,8},{12,10},{14,12},{1,15},{3,1}... | collective-permute-start | bytes 393224 | tf_op jit(solution)/shard_map/ppermute | solution.py:205
  129.3 16.0 %collective-permute-start.9 = (f32[256,128]{1,0:T(8,128)S(1)}, f32[256,128]{1,0:T(8,128)S(1)}, u32[]{:S(2)}, u32[]{:S(2)}) collective-permute-start(f32[256,128]{1,0:T(8,128)S(1)} %get-tuple-element.17), channel_id=1, source_target_pairs={{0,8},{2,10},{4,12},{6,14},{8,0},{10,2},{12,4},{14,6},{1,9},{3,11}... | collective-permute-start | bytes 393224 | tf_op jit(solution)/shard_map/ppermute | solution.py:205
  132.3 13.1 %collective-permute-start.8 = (f32[256,128]{1,0:T(8,128)S(1)}, f32[256,128]{1,0:T(8,128)S(1)}, u32[]{:S(2)}, u32[]{:S(2)}) collective-permute-start(f32[256,128]{1,0:T(8,128)S(1)} %get-tuple-element.18), channel_id=1, source_target_pairs={{0,6},{2,8},{4,10},{6,12},{8,14},{10,0},{12,2},{14,4},{1,7},{3,9},... | collective-permute-start | bytes 393224 | tf_op jit(solution)/shard_map/ppermute | solution.py:205
  132.7 12.6 %collective-permute-start.7 = (f32[256,128]{1,0:T(8,128)S(1)}, f32[256,128]{1,0:T(8,128)}, u32[]{:S(2)}, u32[]{:S(2)}) collective-permute-start(f32[256,128]{1,0:T(8,128)S(1)} %get-tuple-element.19), channel_id=1, source_target_pairs={{0,4},{2,6},{4,8},{6,10},{8,12},{10,14},{12,0},{14,2},{1,5},{3,7},... | collective-permute-start | bytes 393224 | tf_op jit(solution)/shard_map/ppermute | solution.py:205
  147.0 24.8 %collective-permute-start.19 = (f32[256,128]{1,0:T(8,128)S(1)}, f32[256,128]{1,0:T(8,128)S(1)}, u32[]{:S(2)}, u32[]{:S(2)}) collective-permute-start(f32[256,128]{1,0:T(8,128)S(1)} %fusion.13), channel_id=1, source_target_pairs={{0,2},{2,4},{4,6},{6,8},{8,10},{10,12},{12,14},{14,0},{1,3},{3,5},... | collective-permute-start | bytes 393224 | tf_op jit(solution)/shard_map/ppermute | solution.py:205
  148.4 23.3 %collective-permute-start.18 = (f32[256,128]{1,0:T(8,128)S(1)}, f32[256,128]{1,0:T(8,128)S(1)}, u32[]{:S(2)}, u32[]{:S(2)}) collective-permute-start(f32[256,128]{1,0:T(8,128)S(1)} %fusion.13), channel_id=1, source_target_pairs={{0,4},{2,6},{4,8},{6,10},{8,12},{10,14},{12,0},{14,2},{1,5},{3,7},... | collective-permute-start | bytes 393224 | tf_op jit(solution)/shard_map/ppermute | solution.py:205
  149.6 22.1 %collective-permute-start.17 = (f32[256,128]{1,0:T(8,128)S(1)}, f32[256,128]{1,0:T(8,128)S(1)}, u32[]{:S(2)}, u32[]{:S(2)}) collective-permute-start(f32[256,128]{1,0:T(8,128)S(1)} %fusion.13), channel_id=1, source_target_pairs={{0,6},{2,8},{4,10},{6,12},{8,14},{10,0},{12,2},{14,4},{1,7},{3,9},... | collective-permute-start | bytes 393224 | tf_op jit(solution)/shard_map/ppermute | solution.py:205
  151.6 20.1 %collective-permute-start.16 = (f32[256,128]{1,0:T(8,128)S(1)}, f32[256,128]{1,0:T(8,128)S(1)}, u32[]{:S(2)}, u32[]{:S(2)}) collective-permute-start(f32[256,128]{1,0:T(8,128)S(1)} %fusion.13), channel_id=1, source_target_pairs={{0,8},{2,10},{4,12},{6,14},{8,0},{10,2},{12,4},{14,6},{1,9},{3,11}... | collective-permute-start | bytes 393224 | tf_op jit(solution)/shard_map/ppermute | solution.py:205
  160.7 11.0 %collective-permute-start.15 = (f32[256,128]{1,0:T(8,128)S(1)}, f32[256,128]{1,0:T(8,128)S(1)}, u32[]{:S(2)}, u32[]{:S(2)}) collective-permute-start(f32[256,128]{1,0:T(8,128)S(1)} %fusion.13), channel_id=1, source_target_pairs={{0,10},{2,12},{4,14},{6,0},{8,2},{10,4},{12,6},{14,8},{1,11},{3,13... | collective-permute-start | bytes 393224 | tf_op jit(solution)/shard_map/ppermute | solution.py:205
  249.0 9.5 %collective-permute-start.21 = (f32[64,512]{1,0:T(8,128)S(1)}, f32[64,512]{1,0:T(8,128)S(1)}, u32[]{:S(2)}, u32[]{:S(2)}) collective-permute-start(f32[64,512]{1,0:T(8,128)S(1)} %get-tuple-element.6), channel_id=1, source_target_pairs={{0,2},{2,4},{4,6},{6,8},{8,10},{10,12},{12,14},{14,0},{1,3},{3,5},... | collective-permute-start | bytes 393224 | tf_op jit(solution)/shard_map/ppermute | solution.py:205
  255.5 22.3 %collective-permute-start.24 = (f32[64,512]{1,0:T(8,128)}, f32[64,512]{1,0:T(8,128)}, u32[]{:S(2)}, u32[]{:S(2)}) collective-permute-start(f32[64,512]{1,0:T(8,128)} %get-tuple-element.10), channel_id=1, source_target_pairs={{0,8},{2,10},{4,12},{6,14},{8,0},{10,2},{12,4},{14,6},{1,9},{3,11}... | collective-permute-start | bytes 393224 | tf_op jit(solution)/shard_map/ppermute | solution.py:205
  258.4 19.3 %collective-permute-start.23 = (f32[64,512]{1,0:T(8,128)S(1)}, f32[64,512]{1,0:T(8,128)}, u32[]{:S(2)}, u32[]{:S(2)}) collective-permute-start(f32[64,512]{1,0:T(8,128)S(1)} %get-tuple-element.11), channel_id=1, source_target_pairs={{0,6},{2,8},{4,10},{6,12},{8,14},{10,0},{12,2},{14,4},{1,7},{3,9},... | collective-permute-start | bytes 393224 | tf_op jit(solution)/shard_map/ppermute | solution.py:205
  260.5 17.3 %collective-permute-start.22 = (f32[64,512]{1,0:T(8,128)S(1)}, f32[64,512]{1,0:T(8,128)}, u32[]{:S(2)}, u32[]{:S(2)}) collective-permute-start(f32[64,512]{1,0:T(8,128)S(1)} %get-tuple-element.12), channel_id=1, source_target_pairs={{0,4},{2,6},{4,8},{6,10},{8,12},{10,14},{12,0},{14,2},{1,5},{3,7},... | collective-permute-start | bytes 393224 | tf_op jit(solution)/shard_map/ppermute | solution.py:205
  279.1 10.4 %collective-permute-start.28 = (f32[64,512]{1,0:T(8,128)S(1)}, f32[64,512]{1,0:T(8,128)S(1)}, u32[]{:S(2)}, u32[]{:S(2)}) collective-permute-start(f32[64,512]{1,0:T(8,128)S(1)} %fusion.7), channel_id=1, source_target_pairs={{0,14},{2,0},{4,2},{6,4},{8,6},{10,8},{12,10},{14,12},{1,15},{3,1}... | collective-permute-start | bytes 393224 | tf_op jit(solution)/shard_map/ppermute | solution.py:205
  283.2 29.5 %collective-permute-start.34 = (f32[64,512]{1,0:T(8,128)S(1)}, f32[64,512]{1,0:T(8,128)S(1)}, u32[]{:S(2)}, u32[]{:S(2)}) collective-permute-start(f32[64,512]{1,0:T(8,128)S(1)} %fusion.7), channel_id=1, source_target_pairs={{0,2},{2,4},{4,6},{6,8},{8,10},{10,12},{12,14},{14,0},{1,3},{3,5},... | collective-permute-start | bytes 393224 | tf_op jit(solution)/shard_map/ppermute | solution.py:205
  285.2 27.4 %collective-permute-start.33 = (f32[64,512]{1,0:T(8,128)S(1)}, f32[64,512]{1,0:T(8,128)S(1)}, u32[]{:S(2)}, u32[]{:S(2)}) collective-permute-start(f32[64,512]{1,0:T(8,128)S(1)} %fusion.7), channel_id=1, source_target_pairs={{0,4},{2,6},{4,8},{6,10},{8,12},{10,14},{12,0},{14,2},{1,5},{3,7},... | collective-permute-start | bytes 393224 | tf_op jit(solution)/shard_map/ppermute | solution.py:205
  285.2 27.4 %collective-permute-start.32 = (f32[64,512]{1,0:T(8,128)S(1)}, f32[64,512]{1,0:T(8,128)S(1)}, u32[]{:S(2)}, u32[]{:S(2)}) collective-permute-start(f32[64,512]{1,0:T(8,128)S(1)} %fusion.7), channel_id=1, source_target_pairs={{0,6},{2,8},{4,10},{6,12},{8,14},{10,0},{12,2},{14,4},{1,7},{3,9},... | collective-permute-start | bytes 393224 | tf_op jit(solution)/shard_map/ppermute | solution.py:205
  287.6 25.0 %collective-permute-start.31 = (f32[64,512]{1,0:T(8,128)S(1)}, f32[64,512]{1,0:T(8,128)S(1)}, u32[]{:S(2)}, u32[]{:S(2)}) collective-permute-start(f32[64,512]{1,0:T(8,128)S(1)} %fusion.7), channel_id=1, source_target_pairs={{0,8},{2,10},{4,12},{6,14},{8,0},{10,2},{12,4},{14,6},{1,9},{3,11}... | collective-permute-start | bytes 393224 | tf_op jit(solution)/shard_map/ppermute | solution.py:205
  289.5 9.5 %collective-permute-start.29 = (f32[64,512]{1,0:T(8,128)S(1)}, f32[64,512]{1,0:T(8,128)S(1)}, u32[]{:S(2)}, u32[]{:S(2)}) collective-permute-start(f32[64,512]{1,0:T(8,128)S(1)} %fusion.7), channel_id=1, source_target_pairs={{0,12},{2,14},{4,0},{6,2},{8,4},{10,6},{12,8},{14,10},{1,13},{3,15... | collective-permute-start | bytes 393224 | tf_op jit(solution)/shard_map/ppermute | solution.py:205
  299.0 13.6 %collective-permute-start.30 = (f32[64,512]{1,0:T(8,128)S(1)}, f32[64,512]{1,0:T(8,128)S(1)}, u32[]{:S(2)}, u32[]{:S(2)}) collective-permute-start(f32[64,512]{1,0:T(8,128)S(1)} %fusion.7), channel_id=1, source_target_pairs={{0,10},{2,12},{4,14},{6,0},{8,2},{10,4},{12,6},{14,8},{1,11},{3,13... | collective-permute-start | bytes 393224 | tf_op jit(solution)/shard_map/ppermute | solution.py:205
  (16 other events, 141.9 us)
Sparse Core Ops, SparseCore 0:
  204.4 21.4 all-gather.1
